TPU v7x, 512 devices: a whole 4x4x16 slice. The times are simulated.
512 devices in a mesh: dp: 16 (over z), expert: 32 (over y, x, core).
Axes of the slice: x: 4, y: 4, z: 16, core: 2. Of those that a mesh axis runs over, the one named last changes fastest.
Arguments:
- tokens: bfloat16 [65536, 1024], P(('dp', 'expert')), may hold values from -6 to 6
- grad_out: bfloat16 [65536, 1024], P(('dp', 'expert')), may hold values from -6 to 6
- expert_ids: int32 [65536, 2], P(('dp', 'expert')), may hold values from 0 to 31, all different within a row; in each aligned block of 128 rows (0 to 127, 128 to 255, ...) at most 16 rows name the same one
- route_probs: bfloat16 [65536, 2], P(('dp', 'expert')), may hold values from 0.19921875 to 1
- gate_up_weight: bfloat16 [1024, 32, 1536], P('dp', 'expert'), may hold values from -0.1875 to 0.1875
- down_weight: bfloat16 [32, 768, 1024], P('expert'), may hold values from -0.21875 to 0.21875
- gate_up_scale_index: int32 [8, 32, 2], P(None, 'expert'), may hold values from 0 to 15
- down_scale_index: int32 [32, 6], P('expert'), may hold values from 0 to 15
- scale_table: float32 [16], replicated, may hold values from 0.5 to 2
Outputs:
- token_grad: bfloat16 [65536, 1024], P(('dp', 'expert'))
- prob_grad: float32 [65536, 2], P(('dp', 'expert'))
- gate_up_grad: bfloat16 [1024, 32, 1536], P('dp', 'expert')
- down_grad: bfloat16 [32, 768, 1024], P('expert')
Inputs may be any that keep to these rules, and one draw needn't show every extreme that they name: `expert_ids`: each row names two different experts. The 128 rows of one device name one expert at most 16 times, and in every draw some device's rows name some expert exactly 16 times.
All inputs are finite; a program needn't handle non-finite values.
Results may differ from a plain program's by a relative error of at most 0.022.
Values may be sent and summed in bfloat16 or wider, within the bound.
No kernel may reach another device: no remote copies, remote signals or barrier semaphores. Data moves between devices by JAX's collectives and lax.ppermute only.
A program may use at most 64 MiB of HBM per device.

v0:
```python
import jax
import jax.numpy as jnp
from jax import lax
from jax.sharding import PartitionSpec as P

QBLOCK = 128


def lookup(level_index, level_table):
    onehot = (level_index[..., None] == jnp.arange(level_table.shape[0], dtype=jnp.int32)).astype(
        level_table.dtype
    )
    return jnp.sum(onehot * level_table, axis=-1)


def slot_tables(routes, experts, capacity):
    flat_routes = routes.reshape(-1)
    expert_hits = (flat_routes[:, None] == jnp.arange(experts, dtype=jnp.int32)[None, :]).astype(
        jnp.int32
    )
    place = jnp.arange(flat_routes.shape[0], dtype=jnp.int32)
    earlier = (place[None, :] < place[:, None]).astype(jnp.bfloat16)
    before = jnp.dot(
        earlier, expert_hits.astype(jnp.bfloat16), preferred_element_type=jnp.float32
    ).astype(jnp.int32)
    slot_rank = jnp.sum(before * expert_hits, axis=1)
    destination = flat_routes * capacity + slot_rank
    table_hits = destination[:, None] == jnp.arange(experts * capacity, dtype=jnp.int32)[None, :]
    return table_hits.astype(jnp.float32).reshape(routes.shape[0], 2, experts * capacity)


def body(
    tokens,
    grad_out,
    expert_ids,
    route_probs,
    gate_up_weight,
    down_weight,
    gate_up_scale_index,
    down_scale_index,
    scale_table,
):
    high = lax.Precision.HIGHEST
    f32 = jnp.float32
    groups = lax.axis_size("expert")
    tok_dev = tokens.shape[0]
    model_width = tokens.shape[1]
    per_device = down_weight.shape[0]
    hidden = down_weight.shape[1]
    experts = per_device * groups
    capacity = 4 * tok_dev // experts
    slots_all = experts * capacity
    slot_hits = slot_tables(expert_ids, experts, capacity)
    either = (slot_hits[:, 0] + slot_hits[:, 1]).astype(jnp.bfloat16)
    row_shape = (groups, per_device, capacity, model_width)
    send_tokens = (
        jnp.einsum("ts,td->sd", either, tokens, preferred_element_type=f32)
        .astype(jnp.bfloat16)
        .reshape(row_shape)
    )
    send_grads = (
        jnp.einsum("ts,td->sd", either, grad_out, preferred_element_type=f32)
        .astype(jnp.bfloat16)
        .reshape(row_shape)
    )
    send_probs = (
        jnp.einsum("tks,tk->s", slot_hits, route_probs.astype(f32), precision=high)
        .astype(jnp.bfloat16)
        .reshape(row_shape[:3])
    )
    recv_tokens, recv_grads, recv_probs = (
        lax.all_to_all(send_tokens, "expert", split_axis=0, concat_axis=0, tiled=True),
        lax.all_to_all(send_grads, "expert", split_axis=0, concat_axis=0, tiled=True),
        lax.all_to_all(send_probs, "expert", split_axis=0, concat_axis=0, tiled=True),
    )
    level_rows = jnp.repeat(lookup(gate_up_scale_index, scale_table), QBLOCK, axis=0)
    full_scale = jnp.repeat(level_rows, hidden, axis=2)
    down_scale = jnp.repeat(lookup(down_scale_index, scale_table), QBLOCK, axis=1)
    down_eff = (down_weight.astype(f32) * down_scale[:, :, None]).astype(jnp.bfloat16)
    gathered = lax.all_gather(gate_up_weight, "dp", axis=0, tiled=True)
    gate_up_eff = (gathered.astype(f32) * full_scale).astype(jnp.bfloat16)
    projected = jnp.einsum("sjcd,djf->sjcf", recv_tokens, gate_up_eff, preferred_element_type=f32)
    gate_part = projected[..., :hidden]
    up_part = projected[..., hidden:]
    sigmoid_gate = jax.nn.sigmoid(gate_part)
    activated = gate_part * sigmoid_gate
    hidden_rows = (activated * up_part).astype(jnp.bfloat16)
    hidden_grad = jnp.einsum("sjcd,jfd->sjcf", recv_grads, down_eff, preferred_element_type=f32)
    probs_wide = recv_probs.astype(f32)[..., None]
    scaled_grad = probs_wide * hidden_grad
    gate_grad = scaled_grad * up_part * sigmoid_gate * (1.0 + gate_part * (1.0 - sigmoid_gate))
    up_grad = scaled_grad * activated
    joint_grad = jnp.concatenate([gate_grad, up_grad], axis=-1).astype(jnp.bfloat16)
    row_grads = jnp.einsum(
        "sjcf,djf->sjcd", joint_grad, gate_up_eff, preferred_element_type=f32
    ).astype(jnp.bfloat16)
    back_rows = lax.all_to_all(row_grads, "expert", split_axis=0, concat_axis=0, tiled=True)
    token_grad = jnp.dot(
        either, back_rows.reshape(slots_all, model_width), preferred_element_type=f32
    ).astype(jnp.bfloat16)
    expert_out = jnp.einsum("sjcf,jfd->sjcd", hidden_rows, down_eff, preferred_element_type=f32)
    back_out = lax.all_to_all(
        expert_out.astype(jnp.bfloat16), "expert", split_axis=0, concat_axis=0, tiled=True
    ).astype(expert_out.dtype)
    picked = jnp.einsum(
        "tks,sd->tkd", slot_hits, back_out.reshape(slots_all, model_width), precision=high
    )
    prob_grad = jnp.sum(picked * grad_out.astype(f32)[:, None, :], axis=-1)
    weighted = (probs_wide * hidden_rows.astype(f32)).astype(jnp.bfloat16)
    partial_sum = jnp.einsum("sjcd,sjcf->djf", recv_tokens, joint_grad, preferred_element_type=f32)
    gate_up_grad = lax.psum_scatter(
        (partial_sum * full_scale).astype(jnp.bfloat16), "dp", scatter_dimension=0, tiled=True
    )
    down_part = (
        jnp.einsum("sjcf,sjcd->jfd", weighted, recv_grads, preferred_element_type=f32)
        * down_scale[:, :, None]
    )
    down_grad = lax.psum(down_part.astype(jnp.bfloat16), "dp")
    return (token_grad, prob_grad, gate_up_grad, down_grad)


def solution(mesh):
    in_specs = (
        P(("dp", "expert"), None),
        P(("dp", "expert"), None),
        P(("dp", "expert"), None),
        P(("dp", "expert"), None),
        P("dp", "expert", None),
        P("expert", None, None),
        P(None, "expert", None),
        P("expert", None),
        P(),
    )
    out_specs = (
        P(("dp", "expert"), None),
        P(("dp", "expert"), None),
        P("dp", "expert", None),
        P("expert", None, None),
    )
    return jax.shard_map(body, mesh=mesh, in_specs=in_specs, out_specs=out_specs, check_vma=False)
```

profile of v0, /device:TPU:2, one launch (start us, length us, event | category | flops | bytes accessed | tf_op | source)
XLA Modules:
  0.0 353.9 jit_solution(2334480392853353179)
XLA Ops:
  7.2 0.7 all-gather.2.cloned.1.call-update
  7.9 0.8 copy.74
  8.8 0.2 fusion.16
  9.1 0.1 reduce_sum.39
  9.3 0.7 multiply_add_fusion
  10.0 0.9 fusion.34
  10.9 0.7 reshape.246
  11.6 9.4 %all-to-all-start = ((bf16[32,1,16]{2,1,0:T(2,128)(2,1)}), bf16[32,1,16]{2,1,0:T(2,128)(2,1)S(1)}, u32[]{:S(2)}, u32[]{:S(2)}) async-start(bf16[32,1,16]{2,1,0:T(2,128)(2,1)} %reshape.246), calls=%async_computation | async-start | bytes 32768 | tf_op jit(solution)/shard_map/all_to_all | solution.py:74
  21.2 1.4 convolution_convert_fusion.1
  22.6 4.5 %all-to-all-done = bf16[32,1,16]{2,1,0:T(2,128)(2,1)S(1)} async-done(((bf16[32,1,16]{2,1,0:T(2,128)(2,1)}), bf16[32,1,16]{2,1,0:T(2,128)(2,1)S(1)}, u32[]{:S(2)}, u32[]{:S(2)}) %all-to-all-start) | async-done | bytes 1056 | tf_op jit(solution)/shard_map/all_to_all | solution.py:74
  27.2 5.7 %all-to-all-start.2 = ((bf16[32,1,16,1024]{3,2,1,0:T(8,128)(2,1)}), bf16[32,1,16,1024]{3,2,1,0:T(8,128)(2,1)}, u32[]{:S(2)}, u32[]{:S(2)}) async-start(bf16[32,1,16,1024]{3,2,1,0:T(8,128)(2,1)} %bitcast.19), calls=%async_computation.2 | async-start | bytes 2097152 | tf_op jit(solution)/shard_map/all_to_all | solution.py:72
  32.9 0.2 select_reduce_fusion
  33.1 0.2 fusion.43
  33.3 0.7 broadcast_bitcast_fusion.1
  34.0 1.5 convolution_convert_fusion.2
  35.5 55.5 %all-gather.2.cloned.1.call-done = bf16[1024,1,1536]{2,0,1:T(8,128)(2,1)} async-done(((bf16[64,1,1536]{2,0,1:T(8,128)(2,1)}), bf16[1024,1,1536]{2,0,1:T(8,128)(2,1)}) %all-gather.2.cloned.1.call-update) | async-done | bytes 3145744 | tf_op jit(solution)/shard_map/all_gather | solution.py:80
  91.0 3.2 copy.76
  94.2 7.2 %all-to-all-start.1 = ((bf16[32,1,16,1024]{3,2,1,0:T(8,128)(2,1)}), bf16[32,1,16,1024]{3,2,1,0:T(8,128)(2,1)}, u32[]{:S(2)}, u32[]{:S(2)}) async-start(bf16[32,1,16,1024]{3,2,1,0:T(8,128)(2,1)} %bitcast.139), calls=%async_computation.1 | async-start | bytes 2097152 | tf_op jit(solution)/shard_map/all_to_all | solution.py:73
  101.5 0.2 reduce-scatter.4.cloned.1.call-start
  101.7 0.8 broadcast_in_dim.14
  102.5 1.2 fusion.3
  103.7 1.7 copy-done.1
  105.4 1.7 copy-done.2
  107.1 5.1 %convolution_bitcast_fusion = f32[32,1,16,1536]{3,0,2,1:T(8,128)} fusion(bf16[1024,1536,1]{0,1,2:T(8,128)(2,1)S(1)} %fusion.3, bf16[32,1,16,1024]{3,2,1,0:T(8,128)(2,1)} %all-to-all-done.2), kind=kOutput, calls=%fused_computation.4 | convolution fusion | flops 1610612736 | bytes 7340032 | tf_op jit(solution)/shard_map/sjcd,djf->sjcf/dot_general | solution.py:82
  112.2 5.5 %all-to-all-done.1 = bf16[32,1,16,1024]{3,2,1,0:T(8,128)(2,1)} async-done(((bf16[32,1,16,1024]{3,2,1,0:T(8,128)(2,1)}), bf16[32,1,16,1024]{3,2,1,0:T(8,128)(2,1)}, u32[]{:S(2)}, u32[]{:S(2)}) %all-to-all-start.1) | async-done | bytes 1048608 | tf_op jit(solution)/shard_map/all_to_all | solution.py:73
  117.6 5.3 %fusion.31 = (bf16[32,16,768]{2,0,1:T(8,128)(2,1)S(1)}, bf16[32,16,768]{2,0,1:T(8,128)(2,1)S(1)}, bf16[32,1,16,768]{3,0,2,1:T(8,128)(2,1)}) fusion(f32[32,1,16,1536]{3,0,2,1:T(8,128)} %convolution_bitcast_fusion, bf16[32,1,16,1024]{3,2,1,0:T(8,128)(2,1)} %all-to-all-done.1, bf16[1,768,1024]{2,1,0:T(8,128)(2,1)S(1)} %copy-done.11, f32[768]{0:T(1024)S(1)} %copy-done.8, ...), kind=kOutput, calls=%fused_computation.49 | convolution fusion | flops 813957120 | bytes 8131584 | tf_op jit(solution)/shard_map/sjcd,jfd->sjcf/dot_general | solution.py:88
  123.0 3.8 %fusion.17 = f32[1536,1024,1]{1,0,2:T(8,128)S(1)} fusion(bf16[32,16,768]{2,0,1:T(8,128)(2,1)S(1)} %get-tuple-element.25, bf16[32,16,768]{2,0,1:T(8,128)(2,1)S(1)} %get-tuple-element.24, bf16[32,1,16,1024]{3,2,1,0:T(8,128)(2,1)} %all-to-all-done.2), kind=kOutput, calls=%fused_computation.36 | convolution fusion | flops 1613758464 | bytes 8912896 | tf_op jit(solution)/shard_map/sjcd,sjcf->djf/dot_general | solution.py:110
  126.8 1.8 fusion.2
  128.6 3.0 copy.96
  131.6 1.4 copy-done.12
  133.0 0.2 copy-done.14
  133.2 1.1 fusion.12
  134.3 1.6 copy.86
  135.8 5.7 %all-to-all-start.4 = ((bf16[32,1,16,1024]{3,2,1,0:T(8,128)(2,1)}), bf16[32,1,16,1024]{3,2,1,0:T(8,128)(2,1)}, u32[]{:S(2)}, u32[]{:S(2)}) async-start(bf16[32,1,16,1024]{3,2,1,0:T(8,128)(2,1)} %copy.86), calls=%async_computation.4 | async-start | bytes 2097152 | tf_op jit(solution)/shard_map/all_to_all | solution.py:102
  141.6 0.3 all-reduce.2.cloned.1.call-start
  141.8 4.1 %fusion.11 = bf16[1,768,1024]{2,1,0:T(8,128)(2,1)} fusion(f32[768]{0:T(1024)S(1)} %copy-done.8, bf16[32,1,16,1024]{3,2,1,0:T(8,128)(2,1)} %all-to-all-done.1, bf16[32,1,16,768]{3,0,2,1:T(8,128)(2,1)} %get-tuple-element.26, f32[32,16]{0,1:T(8,128)S(1)} %copy.78), kind=kOutput, calls=%fused_computation.23 | convolution fusion | flops 808058880 | bytes 3412992 | tf_op jit(solution)/shard_map/sjcf,sjcd->jfd/dot_general | solution.py:115
  146.0 3.2 fusion.13
  149.2 1.6 copy.85
  150.7 7.1 %all-to-all-done.4 = bf16[32,1,16,1024]{3,2,1,0:T(8,128)(2,1)} async-done(((bf16[32,1,16,1024]{3,2,1,0:T(8,128)(2,1)}), bf16[32,1,16,1024]{3,2,1,0:T(8,128)(2,1)}, u32[]{:S(2)}, u32[]{:S(2)}) %all-to-all-start.4) | async-done | bytes 1048608 | tf_op jit(solution)/shard_map/all_to_all | solution.py:102
  157.8 5.0 %all-to-all-start.3 = ((bf16[32,1,16,1024]{3,2,1,0:T(8,128)(2,1)}), bf16[32,1,16,1024]{3,2,1,0:T(8,128)(2,1)S(1)}, u32[]{:S(2)}, u32[]{:S(2)}) async-start(bf16[32,1,16,1024]{3,2,1,0:T(8,128)(2,1)} %copy.85), calls=%async_computation.3 | async-start | bytes 2097152 | tf_op jit(solution)/shard_map/all_to_all | solution.py:97
  162.9 2.4 fusion.14
  165.3 13.8 %all-to-all-done.3 = bf16[32,1,16,1024]{3,2,1,0:T(8,128)(2,1)S(1)} async-done(((bf16[32,1,16,1024]{3,2,1,0:T(8,128)(2,1)}), bf16[32,1,16,1024]{3,2,1,0:T(8,128)(2,1)S(1)}, u32[]{:S(2)}, u32[]{:S(2)}) %all-to-all-start.3) | async-done | bytes 1048608 | tf_op jit(solution)/shard_map/all_to_all | solution.py:97
  179.1 1.0 convolution_convert_fusion.4
  180.1 22.4 %reduce-scatter.4.cloned.1.call-done = bf16[64,1536]{1,0:T(8,128)(2,1)} async-done(((bf16[1024,1536]{1,0:T(8,128)(2,1)}), bf16[64,1536]{1,0:T(8,128)(2,1)}) %reduce-scatter.4.cloned.1.call-update) | async-done | bytes 196624
  202.5 1.1 copy.97
  203.6 0.8 copy.88
  204.5 140.2 %all-reduce.2.cloned.1.call-done = bf16[1,768,1024]{2,1,0:T(8,128)(2,1)} async-done(((bf16[1,768,1024]{2,1,0:T(8,128)(2,1)}), bf16[1,768,1024]{2,1,0:T(8,128)(2,1)}) %all-reduce.2.cloned.1.call-update) | async-done | bytes 1572880 | tf_op jit(solution)/shard_map/psum | solution.py:118
  344.7 2.7 copy.122
  (49 shorter events, 0.7 us)
Async XLA Ops:
  7.2 14.0 %copy-start = (bf16[128,1024]{1,0:T(8,128)(2,1)S(1)}, bf16[128,1024]{1,0:T(8,128)(2,1)}, u32[]{:S(2)}) copy-start(bf16[128,1024]{1,0:T(8,128)(2,1)} %param.9) | copy-start | bytes 786436
  7.2 83.9 %all-gather.2.cloned.1.call-start = ((), (), s32[]{:S(2)}) async-start(), calls=%async_computation.6 | async-start | bytes 3342336 | tf_op jit(solution)/shard_map/all_gather | solution.py:80
  10.0 11.0 %copy-start.6 = (s32[128,2]{0,1:T(2,128)}, s32[128,2]{0,1:T(2,128)S(1)}, u32[]{:S(2)}) copy-start(s32[128,2]{0,1:T(2,128)S(1)} %multiply_add_fusion) | copy-start | bytes 3076
  11.6 15.6 %all-to-all-start = ((bf16[32,1,16]{2,1,0:T(2,128)(2,1)}), bf16[32,1,16]{2,1,0:T(2,128)(2,1)S(1)}, u32[]{:S(2)}, u32[]{:S(2)}) async-start(bf16[32,1,16]{2,1,0:T(2,128)(2,1)} %reshape.246), calls=%async_computation | async-start | bytes 32768 | tf_op jit(solution)/shard_map/all_to_all | solution.py:74
  21.1 11.8 %copy-start.9 = (s32[8,1,2]{0,2,1:T(2,128)S(1)}, s32[8,1,2]{0,2,1:T(2,128)}, u32[]{:S(2)}) copy-start(s32[8,1,2]{0,2,1:T(2,128)} %param.15) | copy-start | bytes 196
  21.1 11.8 %copy-start.10 = (f32[16]{0:T(128)S(1)}, f32[16]{0:T(128)}, u32[]{:S(2)}) copy-start(f32[16]{0:T(128)} %param.17) | copy-start | bytes 196
  21.1 12.0 %copy-start.13 = (s32[1,6]{1,0:T(1,128)S(1)}, s32[1,6]{1,0:T(1,128)}, u32[]{:S(2)}) copy-start(s32[1,6]{1,0:T(1,128)} %param.16) | copy-start | bytes 76
  21.2 12.9 %copy-start.4 = (bf16[128,1024]{1,0:T(8,128)(2,1)S(1)}, bf16[128,1024]{1,0:T(8,128)(2,1)}, u32[]{:S(2)}) copy-start(bf16[128,1024]{1,0:T(8,128)(2,1)} %param.10) | copy-start | bytes 786436
  27.2 67.1 %all-to-all-start.2 = ((bf16[32,1,16,1024]{3,2,1,0:T(8,128)(2,1)}), bf16[32,1,16,1024]{3,2,1,0:T(8,128)(2,1)}, u32[]{:S(2)}, u32[]{:S(2)}) async-start(bf16[32,1,16,1024]{3,2,1,0:T(8,128)(2,1)} %bitcast.19), calls=%async_computation.2 | async-start | bytes 2097152 | tf_op jit(solution)/shard_map/all_to_all | solution.py:72
  94.2 23.4 %all-to-all-start.1 = ((bf16[32,1,16,1024]{3,2,1,0:T(8,128)(2,1)}), bf16[32,1,16,1024]{3,2,1,0:T(8,128)(2,1)}, u32[]{:S(2)}, u32[]{:S(2)}) async-start(bf16[32,1,16,1024]{3,2,1,0:T(8,128)(2,1)} %bitcast.139), calls=%async_computation.1 | async-start | bytes 2097152 | tf_op jit(solution)/shard_map/all_to_all | solution.py:73
  101.5 101.0 %reduce-scatter.4.cloned.1.call-start = ((), (), s32[]{:S(2)}) async-start(), calls=%async_computation.8 | async-start | bytes 3342336
  102.5 2.9 copy-start.1
  105.3 1.7 copy-start.2
  107.1 10.6 %copy-start.8 = (f32[768]{0:T(1024)S(1)}, f32[768]{0:T(1024)}, u32[]{:S(2)}) copy-start(f32[768]{0:T(1024)} %broadcast_bitcast_fusion.1) | copy-start | bytes 9220
  107.1 10.6 %copy-start.11 = (bf16[1,768,1024]{2,1,0:T(8,128)(2,1)S(1)}, bf16[1,768,1024]{2,1,0:T(8,128)(2,1)}, u32[]{:S(2)}) copy-start(bf16[1,768,1024]{2,1,0:T(8,128)(2,1)} %param.14) | copy-start | bytes 4718596
  117.6 9.2 %slice-start = ((s8[6291456]{0:T(1024)(128)(4,1)}), s8[4194304]{0:T(1024)(128)(4,1)S(1)}, s32[]{:S(2)}) async-start(s8[6291456]{0:T(1024)(128)(4,1)} %bitcast.136), calls=%async_computation.9 | async-start | bytes 8388608
  122.9 3.8 %copy-start.15 = (bf16[32,16,768]{2,0,1:T(8,128)(2,1)}, bf16[32,16,768]{2,0,1:T(8,128)(2,1)S(1)}, u32[]{:S(2)}) copy-start(bf16[32,16,768]{2,0,1:T(8,128)(2,1)S(1)} %get-tuple-element.24) | copy-start | bytes 2359300
  122.9 3.8 %copy-start.16 = (bf16[32,16,768]{2,0,1:T(8,128)(2,1)}, bf16[32,16,768]{2,0,1:T(8,128)(2,1)S(1)}, u32[]{:S(2)}) copy-start(bf16[32,16,768]{2,0,1:T(8,128)(2,1)S(1)} %get-tuple-element.25) | copy-start | bytes 2359300
  123.0 3.9 %slice-start.1 = ((s8[6291456]{0:T(1024)(128)(4,1)}), s8[2097152]{0:T(1024)(128)(4,1)S(1)}, s32[]{:S(2)}) async-start(s8[6291456]{0:T(1024)(128)(4,1)} %bitcast.136), calls=%async_computation.10 | async-start | bytes 4194304
  131.6 1.4 copy-start.12
  131.6 1.6 copy-start.14
  135.8 22.0 %all-to-all-start.4 = ((bf16[32,1,16,1024]{3,2,1,0:T(8,128)(2,1)}), bf16[32,1,16,1024]{3,2,1,0:T(8,128)(2,1)}, u32[]{:S(2)}, u32[]{:S(2)}) async-start(bf16[32,1,16,1024]{3,2,1,0:T(8,128)(2,1)} %copy.86), calls=%async_computation.4 | async-start | bytes 2097152 | tf_op jit(solution)/shard_map/all_to_all | solution.py:102
  141.6 4.4 %copy-start.3 = (bf16[1024,1536,1]{0,1,2:T(8,128)(2,1)S(1)}, bf16[1024,1536,1]{0,1,2:T(8,128)(2,1)}, u32[]{:S(2)}) copy-start(bf16[1024,1536,1]{0,1,2:T(8,128)(2,1)} %copy-done.2) | copy-start | bytes 9437188
  141.6 203.2 %all-reduce.2.cloned.1.call-start = ((), (), s32[]{:S(2)}) async-start(), calls=%async_computation.7 | async-start | bytes 3145728 | tf_op jit(solution)/shard_map/psum | solution.py:118
  149.1 13.7 %copy-start.5 = (bf16[128,1024]{1,0:T(8,128)(2,1)S(1)}, bf16[128,1024]{1,0:T(8,128)(2,1)}, u32[]{:S(2)}) copy-start(bf16[128,1024]{1,0:T(8,128)(2,1)} %param.10) | copy-start | bytes 786436
  149.1 13.8 %copy-start.7 = (s32[128,2]{0,1:T(2,128)S(1)}, s32[128,2]{0,1:T(2,128)}, u32[]{:S(2)}) copy-start(s32[128,2]{0,1:T(2,128)} %copy-done.6) | copy-start | bytes 3076
  157.8 21.3 %all-to-all-start.3 = ((bf16[32,1,16,1024]{3,2,1,0:T(8,128)(2,1)}), bf16[32,1,16,1024]{3,2,1,0:T(8,128)(2,1)S(1)}, u32[]{:S(2)}, u32[]{:S(2)}) async-start(bf16[32,1,16,1024]{3,2,1,0:T(8,128)(2,1)} %copy.85), calls=%async_computation.3 | async-start | bytes 2097152 | tf_op jit(solution)/shard_map/all_to_all | solution.py:97
Sparse Core Ops, SparseCore 0:
  10.1 80.9 all-gather.1
  131.7 70.7 reduce-scatter.3
  205.4 139.2 all-reduce.1
where the time goes:
time: 355 us; the launch traced here: 354 us
  waiting for transfers between devices  250 us (70%)
  starting transfers between devices  33.6 us (9%)
  matrix products  29.9 us (8%)
  local copies, waits for them, and re-layouts  22.4 us (6%)
  between operations  14.1 us (4%)
  other arithmetic  4.22 us (1%)
    psum x1, waiting for transfers between devices, body(): down_grad = lax.psum(down_part.astype(jnp.bfloat16), 'dp')  140 us
    all_gather x1, waiting for transfers between devices, body(): gathered = lax.all_gather(gate_up_weight, 'dp', axis=0, tiled=True)  55.5 us
    unnamed x4, waiting for transfers between devices  23.1 us
    all_to_all x1, waiting for transfers between devices, body(): lax.all_to_all(row_grads, 'expert', split_axis=0, concat_axis=0, tiled=True)  13.8 us
    unnamed x45, local copies, waits for them, and re-layouts  13.5 us
    all_to_all x1, starting transfers between devices, body(): lax.all_to_all(send_probs, 'expert', split_axis=0, concat_axis=0, tiled=T...  9.4 us
    all_to_all x1, starting transfers between devices, body(): lax.all_to_all(send_grads, 'expert', split_axis=0, concat_axis=0, tiled=T...  7.21 us
    all_to_all x1, waiting for transfers between devices, body(): lax.all_to_all(expert_out.astype(jnp.bfloat16), 'expert', split_axis=0, c...  7.1 us
  transfers between devices with their start and end apart: 8, of which 7 were waited for; matrix products, arithmetic and copies ran while one was open for 10% of the time, Pallas kernels for 0%

commit v1 on v0

--- a/solution.py
+++ b/solution.py
@@ -2,6 +2,7 @@
 import jax.numpy as jnp
 from jax import lax
 from jax.sharding import PartitionSpec as P
+from jax.lax import all_to_all, axis_size
 
 QBLOCK = 128
 
@@ -77,7 +78,15 @@
     full_scale = jnp.repeat(level_rows, hidden, axis=2)
     down_scale = jnp.repeat(lookup(down_scale_index, scale_table), QBLOCK, axis=1)
     down_eff = (down_weight.astype(f32) * down_scale[:, :, None]).astype(jnp.bfloat16)
-    gathered = lax.all_gather(gate_up_weight, "dp", axis=0, tiled=True)
+    gathered = jnp.concatenate(
+        all_to_all(
+            jnp.stack([gate_up_weight for _ in range(axis_size("dp"))]),
+            split_axis=0,
+            concat_axis=0,
+            axis_name="dp",
+        ),
+        axis=0,
+    )
     gate_up_eff = (gathered.astype(f32) * full_scale).astype(jnp.bfloat16)
     projected = jnp.einsum("sjcd,djf->sjcf", recv_tokens, gate_up_eff, preferred_element_type=f32)
     gate_part = projected[..., :hidden]

time: 355 us -> 475 us (1.34)
  waiting for transfers between devices: 250 us -> 318 us
  local copies, waits for them, and re-layouts: 22.4 us -> 42.2 us
  blocking collectives: 0 us -> 14.8 us
  other arithmetic: 4.22 us -> 17.2 us
  starting transfers between devices: 33.6 us -> 38.4 us
    all_to_all x1, waiting for transfers between devices: 4.52 us -> 138 us  [body(): all_to_all(jnp.stack([gate_up_weight for _ in range(axis_size('dp'))]), s...]
    all_gather x1 -> x0, waiting for transfers between devices: 55.5 us -> none  [body(): gathered = lax.all_gather(gate_up_weight, 'dp', axis=0, tiled=True)]
    all_to_all x0 -> x1, blocking collectives: none -> 14.8 us  [body(): lax.all_to_all(send_probs, 'expert', split_axis=0, concat_axis=0, tiled=T...]
    convert_element_type x0 -> x2, local copies, waits for them, and re-layouts: none -> 13.4 us  [body(): gate_up_eff = (gathered.astype(f32) * full_scale).astype(jnp.bfloat16)]
    convert_element_type x0 -> x2, other arithmetic: none -> 11.3 us  [body(): gate_up_eff = (gathered.astype(f32) * full_scale).astype(jnp.bfloat16)]
    all_to_all x1, waiting for transfers between devices: 5.47 us -> 0.01 us  [body(): lax.all_to_all(send_grads, 'expert', split_axis=0, concat_axis=0, tiled=T...]
    unnamed x4 -> x3, waiting for transfers between devices: 23.1 us -> 19.8 us
    unnamed x45 -> x35, local copies, waits for them, and re-layouts: 13.5 us -> 15.2 us
  transfers between devices with their start and end apart: 8 -> 7, of which waited for: 7 -> 6; matrix products, arithmetic and copies ran while one was open for 10% -> 13% of each run, Pallas kernels for 0% -> 0%
where the time goes in v1:
time: 475 us; the launch traced here: 474 us
  waiting for transfers between devices  318 us (67%)
  local copies, waits for them, and re-layouts  42.2 us (9%)
  starting transfers between devices  38.4 us (8%)
  matrix products  29.3 us (6%)
  other arithmetic  17.2 us (4%)
  blocking collectives  14.8 us (3%)
  between operations  14.3 us (3%)
    psum x1, waiting for transfers between devices, body(): down_grad = lax.psum(down_part.astype(jnp.bfloat16), 'dp')  140 us
    all_to_all x1, waiting for transfers between devices, body(): all_to_all(jnp.stack([gate_up_weight for _ in range(axis_size('dp'))]), s...  138 us
    unnamed x3, waiting for transfers between devices  19.8 us
    unnamed x35, local copies, waits for them, and re-layouts  15.2 us
    all_to_all x1, blocking collectives, body(): lax.all_to_all(send_probs, 'expert', split_axis=0, concat_axis=0, tiled=T...  14.8 us
    all_to_all x1, starting transfers between devices, body(): all_to_all(jnp.stack([gate_up_weight for _ in range(axis_size('dp'))]), s...  14 us
    all_to_all x1, waiting for transfers between devices, body(): lax.all_to_all(row_grads, 'expert', split_axis=0, concat_axis=0, tiled=True)  13.7 us
    convert_element_type x2, local copies, waits for them, and re-layouts, body(): gate_up_eff = (gathered.astype(f32) * full_scale).astype(jnp.bfloat16)  13.4 us
  transfers between devices with their start and end apart: 7, of which 6 were waited for; matrix products, arithmetic and copies ran while one was open for 13% of the time, Pallas kernels for 0%

profile of v1, /device:TPU:2, one launch (start us, length us, event | category | flops | bytes accessed | tf_op | source)
XLA Modules:
  0.0 473.8 jit_solution(16496788401280869051)
XLA Ops:
  7.2 0.8 copy.69
  8.2 0.2 fusion.22
  8.6 0.7 multiply_add_fusion
  9.3 0.9 fusion.40
  10.3 14.8 %all_to_all.30 = bf16[32,1,16]{2,1,0:T(2,128)(2,1)S(1)} all-to-all(bf16[32,1,16]{2,1,0:T(2,128)(2,1)S(1)} %reshape.285), channel_id=1, replica_groups=mesh['dp'=16,'expert'=32] {'expert'}, dimensions={0} | all-to-all | bytes 2048 | tf_op jit(solution)/shard_map/all_to_all | solution.py:75
  25.1 2.9 stack.2
  27.9 14.0 %all-to-all-start = ((bf16[16,64,1,1536]{3,1,2,0:T(8,128)(2,1)}), bf16[16,64,1,1536]{3,1,2,0:T(8,128)(2,1)S(1)}, u32[]{:S(2)}, u32[]{:S(2)}) async-start(bf16[16,64,1,1536]{3,1,2,0:T(8,128)(2,1)} %stack.2), calls=%async_computation | async-start | bytes 6291456 | tf_op jit(solution)/shard_map/all_to_all | solution.py:82
  42.1 1.4 convolution_convert_fusion
  43.5 137.8 %all-to-all-done = bf16[16,64,1,1536]{3,1,2,0:T(8,128)(2,1)S(1)} async-done(((bf16[16,64,1,1536]{3,1,2,0:T(8,128)(2,1)}), bf16[16,64,1,1536]{3,1,2,0:T(8,128)(2,1)S(1)}, u32[]{:S(2)}, u32[]{:S(2)}) %all-to-all-start) | async-done | bytes 3145760 | tf_op jit(solution)/shard_map/all_to_all | solution.py:82
  181.3 5.7 %all-to-all-start.3 = ((bf16[32,1,16,1024]{3,2,1,0:T(8,128)(2,1)}), bf16[32,1,16,1024]{3,2,1,0:T(8,128)(2,1)}, u32[]{:S(2)}, u32[]{:S(2)}) async-start(bf16[32,1,16,1024]{3,2,1,0:T(8,128)(2,1)} %bitcast.141), calls=%async_computation.3 | async-start | bytes 2097152 | tf_op jit(solution)/shard_map/all_to_all | solution.py:73
  187.0 1.4 select_reduce_fusion
  188.4 1.3 copy.71
  189.8 1.5 broadcast_in_dim.14
  191.3 1.8 copy.88
  193.2 0.9 fusion.49
  194.0 0.7 broadcast_bitcast_fusion
  194.7 1.5 convolution_convert_fusion.1
  196.2 5.4 %reshape.276 = f32[1024,2,768]{2,1,0:T(2,128)} reshape(bf16[16,64,1,1536]{3,1,2,0:T(8,128)(2,1)S(1)} %all-to-all-done) | data formatting | bytes 9437184 | tf_op jit(solution)/shard_map/convert_element_type | solution.py:90
  201.7 1.6 all-to-all-done.3
  203.3 5.9 %all-to-all-start.2 = ((bf16[32,1,16,1024]{3,2,1,0:T(8,128)(2,1)}), bf16[32,1,16,1024]{3,2,1,0:T(8,128)(2,1)}, u32[]{:S(2)}, u32[]{:S(2)}) async-start(bf16[32,1,16,1024]{3,2,1,0:T(8,128)(2,1)} %bitcast.142), calls=%async_computation.2 | async-start | bytes 2097152 | tf_op jit(solution)/shard_map/all_to_all | solution.py:74
  209.2 0.2 reduce-scatter.4.cloned.1.call-start
  209.4 7.3 %multiply_convert_fusion = bf16[1024,2,768]{2,1,0:T(2,128)(2,1)} fusion(f32[1024,2,768]{2,1,0:T(2,128)} %reshape.276, f32[1024,2]{1,0:T(8,128)} %bitcast.139), kind=kLoop, calls=%fused_computation.4 | loop fusion | flops 3145728 | bytes 9445376 | tf_op jit(solution)/shard_map/convert_element_type | solution.py:90
  216.7 8.0 %reshape.280 = bf16[1024,1536,1]{1,0,2:T(8,128)(2,1)} reshape(bf16[1024,2,768]{2,1,0:T(2,128)(2,1)} %multiply_convert_fusion) | data formatting | bytes 6291456 | tf_op jit(solution)/shard_map/convert_element_type | solution.py:90
  224.7 5.7 %convolution_bitcast_fusion = f32[32,1,16,1536]{3,0,2,1:T(8,128)} fusion(bf16[1024,1536,1]{1,0,2:T(8,128)(2,1)} %reshape.280, bf16[32,1,16,1024]{3,2,1,0:T(8,128)(2,1)} %all-to-all-done.3), kind=kOutput, calls=%fused_computation.5 | convolution fusion | flops 1610612736 | bytes 7340032 | tf_op jit(solution)/shard_map/sjcd,djf->sjcf/dot_general | solution.py:91
  230.4 5.6 %fusion.37 = (bf16[32,16,768]{2,0,1:T(8,128)(2,1)S(1)}, bf16[32,16,768]{2,0,1:T(8,128)(2,1)S(1)}, bf16[32,1,16,768]{3,0,2,1:T(8,128)(2,1)}) fusion(f32[32,1,16,1536]{3,0,2,1:T(8,128)} %convolution_bitcast_fusion, bf16[32,1,16,1024]{3,2,1,0:T(8,128)(2,1)} %all-to-all-done.2, bf16[1,768,1024]{2,1,0:T(8,128)(2,1)} %param.14, f32[768]{0:T(1024)S(1)} %copy-done.7, ...), kind=kOutput, calls=%fused_computation.51 | convolution fusion | flops 813957120 | bytes 8131584 | tf_op jit(solution)/shard_map/sjcd,jfd->sjcf/dot_general | solution.py:97
  236.1 3.8 fusion.23
  239.9 0.8 broadcast_in_dim.32.clone
  240.7 2.8 fusion.2
  243.5 4.7 %copy.86 = bf16[1024,1536]{1,0:T(8,128)(2,1)} copy(bf16[1024,1536]{0,1:T(8,128)(2,1)} %fusion.2) | data formatting | bytes 6291456
  248.2 2.7 broadcast_in_dim.32
  251.0 3.1 copy.89
  254.1 1.1 fusion.16
  255.2 1.6 copy.79
  256.8 7.4 %all-to-all-start.5 = ((bf16[32,1,16,1024]{3,2,1,0:T(8,128)(2,1)}), bf16[32,1,16,1024]{3,2,1,0:T(8,128)(2,1)}, u32[]{:S(2)}, u32[]{:S(2)}) async-start(bf16[32,1,16,1024]{3,2,1,0:T(8,128)(2,1)} %copy.79), calls=%async_computation.5 | async-start | bytes 2097152 | tf_op jit(solution)/shard_map/all_to_all | solution.py:111
  264.3 3.8 fusion.15
  268.1 4.0 fusion.1
  272.1 1.8 fusion.17
  274.0 1.6 copy.78
  275.5 4.8 %all-to-all-done.5 = bf16[32,1,16,1024]{3,2,1,0:T(8,128)(2,1)} async-done(((bf16[32,1,16,1024]{3,2,1,0:T(8,128)(2,1)}), bf16[32,1,16,1024]{3,2,1,0:T(8,128)(2,1)}, u32[]{:S(2)}, u32[]{:S(2)}) %all-to-all-start.5) | async-done | bytes 1048608 | tf_op jit(solution)/shard_map/all_to_all | solution.py:111
  280.4 5.0 %all-to-all-start.4 = ((bf16[32,1,16,1024]{3,2,1,0:T(8,128)(2,1)}), bf16[32,1,16,1024]{3,2,1,0:T(8,128)(2,1)S(1)}, u32[]{:S(2)}, u32[]{:S(2)}) async-start(bf16[32,1,16,1024]{3,2,1,0:T(8,128)(2,1)} %copy.78), calls=%async_computation.4 | async-start | bytes 2097152 | tf_op jit(solution)/shard_map/all_to_all | solution.py:106
  285.5 2.4 fusion.20
  287.9 13.7 %all-to-all-done.4 = bf16[32,1,16,1024]{3,2,1,0:T(8,128)(2,1)S(1)} async-done(((bf16[32,1,16,1024]{3,2,1,0:T(8,128)(2,1)}), bf16[32,1,16,1024]{3,2,1,0:T(8,128)(2,1)S(1)}, u32[]{:S(2)}, u32[]{:S(2)}) %all-to-all-start.4) | async-done | bytes 1048608 | tf_op jit(solution)/shard_map/all_to_all | solution.py:106
  301.6 1.0 convolution_convert_fusion.3
  302.7 19.8 %reduce-scatter.4.cloned.1.call-done = bf16[64,1536]{1,0:T(8,128)(2,1)} async-done(((bf16[1024,1536]{1,0:T(8,128)(2,1)}), bf16[64,1536]{1,0:T(8,128)(2,1)}) %reduce-scatter.4.cloned.1.call-update) | async-done | bytes 196624
  322.4 1.1 copy.87
  323.6 0.8 copy.82
  324.4 139.9 %all-reduce.2.cloned.1.call-done = bf16[1,768,1024]{2,1,0:T(8,128)(2,1)} async-done(((bf16[1,768,1024]{2,1,0:T(8,128)(2,1)}), bf16[1,768,1024]{2,1,0:T(8,128)(2,1)}) %all-reduce.2.cloned.1.call-update) | async-done | bytes 1572880 | tf_op jit(solution)/shard_map/psum | solution.py:127
  464.3 2.7 copy.111
  (42 shorter events, 0.8 us)
Async XLA Ops:
  7.2 34.9 %copy-start = (bf16[128,1024]{1,0:T(8,128)(2,1)S(1)}, bf16[128,1024]{1,0:T(8,128)(2,1)}, u32[]{:S(2)}) copy-start(bf16[128,1024]{1,0:T(8,128)(2,1)} %param.9) | copy-start | bytes 786436
  9.3 32.6 %copy-start.5 = (s32[128,2]{0,1:T(2,128)}, s32[128,2]{0,1:T(2,128)S(1)}, u32[]{:S(2)}) copy-start(s32[128,2]{0,1:T(2,128)S(1)} %multiply_add_fusion) | copy-start | bytes 3076
  27.9 153.4 %all-to-all-start = ((bf16[16,64,1,1536]{3,1,2,0:T(8,128)(2,1)}), bf16[16,64,1,1536]{3,1,2,0:T(8,128)(2,1)S(1)}, u32[]{:S(2)}, u32[]{:S(2)}) async-start(bf16[16,64,1,1536]{3,1,2,0:T(8,128)(2,1)} %stack.2), calls=%async_computation | async-start | bytes 6291456 | tf_op jit(solution)/shard_map/all_to_all | solution.py:82
  43.5 151.2 %copy-start.2 = (bf16[128,1024]{1,0:T(8,128)(2,1)S(1)}, bf16[128,1024]{1,0:T(8,128)(2,1)}, u32[]{:S(2)}) copy-start(bf16[128,1024]{1,0:T(8,128)(2,1)} %param.10) | copy-start | bytes 786436
  181.3 22.0 %all-to-all-start.3 = ((bf16[32,1,16,1024]{3,2,1,0:T(8,128)(2,1)}), bf16[32,1,16,1024]{3,2,1,0:T(8,128)(2,1)}, u32[]{:S(2)}, u32[]{:S(2)}) async-start(bf16[32,1,16,1024]{3,2,1,0:T(8,128)(2,1)} %bitcast.141), calls=%async_computation.3 | async-start | bytes 2097152 | tf_op jit(solution)/shard_map/all_to_all | solution.py:73
  203.3 27.1 %all-to-all-start.2 = ((bf16[32,1,16,1024]{3,2,1,0:T(8,128)(2,1)}), bf16[32,1,16,1024]{3,2,1,0:T(8,128)(2,1)}, u32[]{:S(2)}, u32[]{:S(2)}) async-start(bf16[32,1,16,1024]{3,2,1,0:T(8,128)(2,1)} %bitcast.142), calls=%async_computation.2 | async-start | bytes 2097152 | tf_op jit(solution)/shard_map/all_to_all | solution.py:74
  209.2 113.2 %reduce-scatter.4.cloned.1.call-start = ((), (), s32[]{:S(2)}) async-start(), calls=%async_computation.8 | async-start | bytes 3342336
  224.7 5.7 %copy-start.7 = (f32[768]{0:T(1024)S(1)}, f32[768]{0:T(1024)}, u32[]{:S(2)}) copy-start(f32[768]{0:T(1024)} %broadcast_bitcast_fusion) | copy-start | bytes 9220
  236.1 3.8 copy-start.10
  236.1 3.8 copy-start.12
  236.1 3.8 copy-start.4
  251.0 3.1 copy-start.8
  251.0 3.1 copy-start.9
  256.8 23.6 %all-to-all-start.5 = ((bf16[32,1,16,1024]{3,2,1,0:T(8,128)(2,1)}), bf16[32,1,16,1024]{3,2,1,0:T(8,128)(2,1)}, u32[]{:S(2)}, u32[]{:S(2)}) async-start(bf16[32,1,16,1024]{3,2,1,0:T(8,128)(2,1)} %copy.79), calls=%async_computation.5 | async-start | bytes 2097152 | tf_op jit(solution)/shard_map/all_to_all | solution.py:111
  264.2 200.1 %all-reduce.2.cloned.1.call-start = ((), (), s32[]{:S(2)}) async-start(), calls=%async_computation.7 | async-start | bytes 3145728 | tf_op jit(solution)/shard_map/psum | solution.py:127
  268.1 4.0 copy-start.11
  268.1 4.0 copy-start.13
  274.0 11.5 %copy-start.3 = (bf16[128,1024]{1,0:T(8,128)(2,1)S(1)}, bf16[128,1024]{1,0:T(8,128)(2,1)}, u32[]{:S(2)}) copy-start(bf16[128,1024]{1,0:T(8,128)(2,1)} %param.10) | copy-start | bytes 786436
  274.0 11.5 %copy-start.6 = (s32[128,2]{0,1:T(2,128)S(1)}, s32[128,2]{0,1:T(2,128)}, u32[]{:S(2)}) copy-start(s32[128,2]{0,1:T(2,128)} %copy-done.5) | copy-start | bytes 3076
  280.4 21.3 %all-to-all-start.4 = ((bf16[32,1,16,1024]{3,2,1,0:T(8,128)(2,1)}), bf16[32,1,16,1024]{3,2,1,0:T(8,128)(2,1)S(1)}, u32[]{:S(2)}, u32[]{:S(2)}) async-start(bf16[32,1,16,1024]{3,2,1,0:T(8,128)(2,1)} %copy.78), calls=%async_computation.4 | async-start | bytes 2097152 | tf_op jit(solution)/shard_map/all_to_all | solution.py:106
  285.5 181.4 %copy-start.1 = (bf16[128,1024]{1,0:T(8,128)(2,1)S(1)}, bf16[128,1024]{1,0:T(8,128)(2,1)}, u32[]{:S(2)}) copy-start(bf16[128,1024]{1,0:T(8,128)(2,1)} %param.9) | copy-start | bytes 786436
Sparse Core Ops, SparseCore 0:
  248.4 74.0 reduce-scatter.3
  325.3 138.8 all-reduce.1
